TPU v7x, 256 devices: a whole 4x4x8 slice. The times are simulated.
256 devices in a mesh: series: 32 (over z_hi, x, core), tm: 8 (over z_lo, y).
Axes of the slice: x: 4, y: 4, z: 8 (z_hi: 4, z_lo: 2; z = z_hi * 2 + z_lo), core: 2. Of those that a mesh axis runs over, the one named last changes fastest.
Arguments:
- series_data: bfloat16 [128, 1024, 1024], P('series', 'tm'), may hold values from -6 to 6
- group_ids: int32 [128], replicated, may hold values from 0 to 95, never falling along the last dimension, each value on 1 to 4 neighbouring positions
- group_query: bfloat16 [1024, 512], replicated, may hold values from -1.5 to 1.5
- group_key: bfloat16 [1024, 512], replicated, may hold values from -1.5 to 1.5
- group_value: bfloat16 [1024, 512], replicated, may hold values from -0.1875 to 0.1875
- group_out: bfloat16 [512, 1024], replicated, may hold values from -0.25 to 0.25
- time_query: bfloat16 [1024, 512], replicated, may hold values from -1.5 to 1.5
- time_key: bfloat16 [1024, 512], replicated, may hold values from -1.5 to 1.5
- time_value: bfloat16 [1024, 512], replicated, may hold values from -0.1875 to 0.1875
- time_out: bfloat16 [512, 1024], replicated, may hold values from -0.25 to 0.25
Outputs:
- layer_out: bfloat16 [128, 1024, 1024], P('series', 'tm')
Inputs may be any that keep to these rules, and one draw needn't show every extreme that they name: `group_ids`: group numbers never fall along the series; each group holds 1 to 4 series, one exactly 4.
All inputs are finite; a program needn't handle non-finite values.
Results may differ from a plain program's by a relative error of at most 0.0065.
Values may be sent and summed in bfloat16 or wider, within the bound.
No kernel may reach another device: no remote copies, remote signals or barrier semaphores. Data moves between devices by JAX's collectives and lax.ppermute only.
A program may use at most 128 MiB of HBM per device.

v0:
```python
import jax
import jax.numpy as jnp
from jax import lax
from jax.sharding import PartitionSpec as P

HEADS = 8
HEAD_DIM = 64


def rms_norm(values):
    wide = values.astype(jnp.float32)
    return wide * lax.rsqrt(jnp.mean(wide * wide, axis=-1, keepdims=True) + 1e-06)


def project(normed, weight):
    leading = normed.shape[:-1]
    result = jnp.dot(
        normed.reshape(-1, normed.shape[-1]), weight, preferred_element_type=jnp.float32
    )
    return result.reshape(leading + (weight.shape[1],))


def rotate(values, positions):
    halfway = values.shape[-1] // 2
    freqs = 10000.0 ** (-jnp.arange(halfway, dtype=jnp.float32) / halfway)
    angles = positions.astype(jnp.float32)[:, None] * freqs[None, :]
    cosine = jnp.cos(angles)[None, :, None, :]
    sine = jnp.sin(angles)[None, :, None, :]
    first = values[..., :halfway]
    second = values[..., halfway:]
    return jnp.concatenate(
        [first * cosine - second * sine, first * sine + second * cosine], axis=-1
    )


def group_attend(queries, keys, values, query_ids, key_ids):
    rows, spots, inner = queries.shape
    count = keys.shape[0]
    query_h = queries.reshape(rows, spots, HEADS, HEAD_DIM)
    key_h = keys.reshape(count, spots, HEADS, HEAD_DIM)
    value_h = values.reshape(count, spots, HEADS, HEAD_DIM)
    scores = jnp.einsum(
        "sphd,jphd->phsj", query_h, key_h, preferred_element_type=jnp.float32
    ) * HEAD_DIM ** (-0.5)
    allowed = query_ids[:, None] == key_ids[None, :]
    scores = jnp.where(allowed[None, None], scores, -1e30)
    row_top = jnp.max(scores, axis=-1, keepdims=True)
    weights = jnp.where(allowed[None, None], jnp.exp(scores - row_top), 0.0)
    totals = jnp.sum(weights, axis=-1)
    mixed = jnp.einsum(
        "phsj,jphd->sphd", weights.astype(jnp.bfloat16), value_h, preferred_element_type=jnp.float32
    )
    mixed = mixed / jnp.transpose(totals, (2, 0, 1))[..., None]
    return mixed.reshape(rows, spots, inner).astype(jnp.bfloat16)


def on_device(
    series_data,
    group_ids,
    group_query,
    group_key,
    group_value,
    group_out,
    time_query,
    time_key,
    time_value,
    time_out,
):
    s_dev, pt_dev, feature = series_data.shape
    inner = HEADS * HEAD_DIM
    factor = HEAD_DIM ** (-0.5)
    normed_g = rms_norm(series_data).astype(jnp.bfloat16)
    query_g = project(normed_g, group_query).astype(jnp.bfloat16)
    key_g = project(normed_g, group_key).astype(jnp.bfloat16)
    value_g = project(normed_g, group_value).astype(jnp.bfloat16)
    query_r, key_r, value_r = (
        lax.all_to_all(query_g, "series", split_axis=1, concat_axis=0, tiled=True),
        lax.all_to_all(key_g, "series", split_axis=1, concat_axis=0, tiled=True),
        lax.all_to_all(value_g, "series", split_axis=1, concat_axis=0, tiled=True),
    )
    mixed_r = group_attend(query_r, key_r, value_r, group_ids, group_ids)
    mixed_g = lax.all_to_all(mixed_r, "series", split_axis=0, concat_axis=1, tiled=True)
    middle = (series_data.astype(jnp.float32) + project(mixed_g, group_out)).astype(jnp.bfloat16)
    normed_t = rms_norm(middle).astype(jnp.bfloat16)
    positions = lax.axis_index("tm") * pt_dev + jnp.arange(pt_dev, dtype=jnp.int32)
    query_t = rotate(
        project(normed_t, time_query).reshape(s_dev, pt_dev, HEADS, HEAD_DIM), positions
    ).astype(jnp.bfloat16)
    key_t = rotate(
        project(normed_t, time_key).reshape(s_dev, pt_dev, HEADS, HEAD_DIM), positions
    ).astype(jnp.bfloat16)
    value_t = project(normed_t, time_value).astype(jnp.bfloat16)
    key_flat = key_t.reshape(s_dev, pt_dev, inner)
    row_top = jnp.full((s_dev, HEADS, pt_dev), -1e30, jnp.float32)
    key_part = lax.all_gather(key_flat, "tm", axis=1, tiled=True)
    value_part = lax.all_gather(value_t, "tm", axis=1, tiled=True)
    count = key_part.shape[1]
    key_h = key_part.reshape(s_dev, count, HEADS, HEAD_DIM)
    value_h = value_part.reshape(s_dev, count, HEADS, HEAD_DIM)
    scores = (
        jnp.einsum("sqhd,skhd->shqk", query_t, key_h, preferred_element_type=jnp.float32) * factor
    )
    new_top = jnp.maximum(row_top, jnp.max(scores, axis=-1))
    weights = jnp.exp(scores - new_top[..., None])
    totals = jnp.sum(weights, axis=-1)
    update = jnp.einsum(
        "shqk,skhd->shqd", weights.astype(jnp.bfloat16), value_h, preferred_element_type=jnp.float32
    )
    accum = update
    row_top, totals, accum = (new_top, totals, accum)
    mixed = accum / totals[..., None]
    mixed_t = jnp.transpose(mixed, (0, 2, 1, 3)).reshape(s_dev, pt_dev, inner).astype(jnp.bfloat16)
    return (middle.astype(jnp.float32) + project(mixed_t, time_out)).astype(jnp.bfloat16)


def solution(mesh):
    placed = (P("series", "tm", None), P(), P(), P(), P(), P(), P(), P(), P(), P())
    return jax.shard_map(
        on_device, mesh=mesh, in_specs=placed, out_specs=P("series", "tm", None), check_vma=False
    )
```

profile of v0, /device:TPU:128, one launch (start us, length us, event | category | flops | bytes accessed | tf_op | source)
XLA Modules:
  0.0 265.7 jit_solution(1451091682312194021)
XLA Ops:
  6.5 1.6 fusion.7
  8.2 2.4 convolution_convert_fusion.2
  10.5 1.2 copy.35
  11.7 9.8 %all-to-all-start.1 = ((bf16[4,128,512]{2,0,1:T(4,128)(2,1)}), bf16[4,128,512]{2,0,1:T(4,128)(2,1)S(1)}, u32[]{:S(2)}, u32[]{:S(2)}) async-start(bf16[4,128,512]{2,0,1:T(4,128)(2,1)} %copy.35), calls=%async_computation.1 | async-start | bytes 1048576 | tf_op jit(solution)/shard_map/all_to_all | solution.py:77
  21.6 2.0 convolution_convert_fusion.1
  23.6 1.2 copy.37
  24.8 11.3 %all-to-all-done.1 = bf16[4,128,512]{2,0,1:T(4,128)(2,1)S(1)} async-done(((bf16[4,128,512]{2,0,1:T(4,128)(2,1)}), bf16[4,128,512]{2,0,1:T(4,128)(2,1)S(1)}, u32[]{:S(2)}, u32[]{:S(2)}) %all-to-all-start.1) | async-done | bytes 524320 | tf_op jit(solution)/shard_map/all_to_all | solution.py:77
  36.1 8.0 %all-to-all-start.2 = ((bf16[4,128,512]{2,0,1:T(4,128)(2,1)}), bf16[4,128,512]{2,0,1:T(4,128)(2,1)S(1)}, u32[]{:S(2)}, u32[]{:S(2)}) async-start(bf16[4,128,512]{2,0,1:T(4,128)(2,1)} %copy.37), calls=%async_computation.2 | async-start | bytes 1048576 | tf_op jit(solution)/shard_map/all_to_all | solution.py:78
  44.1 2.0 convolution_convert_fusion.3
  47.3 11.7 %all-to-all-done.2 = bf16[4,128,512]{2,0,1:T(4,128)(2,1)S(1)} async-done(((bf16[4,128,512]{2,0,1:T(4,128)(2,1)}), bf16[4,128,512]{2,0,1:T(4,128)(2,1)S(1)}, u32[]{:S(2)}, u32[]{:S(2)}) %all-to-all-start.2) | async-done | bytes 524320 | tf_op jit(solution)/shard_map/all_to_all | solution.py:78
  59.0 8.2 %all-to-all-start = ((bf16[4,128,512]{2,0,1:T(4,128)(2,1)}), bf16[4,128,512]{2,0,1:T(4,128)(2,1)S(1)}, u32[]{:S(2)}, u32[]{:S(2)}) async-start(bf16[4,128,512]{2,0,1:T(4,128)(2,1)} %copy.33), calls=%async_computation | async-start | bytes 1048576 | tf_op jit(solution)/shard_map/all_to_all | solution.py:79
  67.6 1.5 reshape.173
  69.3 1.5 reshape.174
  70.8 10.7 %all-to-all-done = bf16[4,128,512]{2,0,1:T(4,128)(2,1)S(1)} async-done(((bf16[4,128,512]{2,0,1:T(4,128)(2,1)}), bf16[4,128,512]{2,0,1:T(4,128)(2,1)S(1)}, u32[]{:S(2)}, u32[]{:S(2)}) %all-to-all-start) | async-done | bytes 524320 | tf_op jit(solution)/shard_map/all_to_all | solution.py:79
  81.8 1.5 reshape.172
  83.3 3.7 %fusion.53 = (f32[4,8,128]{2,1,0:T(8,128)S(1)}, bf16[4,8,128,128]{2,3,1,0:T(8,128)(2,1)}) fusion(pred[128,128]{0,1:T(8,128)(4,1)S(1)} %broadcast_compare_fusion, bf16[128,4,8,64]{3,2,1,0:T(8,128)(2,1)} %reshape.174, bf16[128,4,8,64]{3,2,1,0:T(8,128)(2,1)S(1)} %copy-done.3), kind=kOutput, calls=%fused_computation.74 | convolution fusion | flops 70254720 | bytes 2129920 | tf_op jit(solution)/shard_map/sub | solution.py:48
  87.0 1.8 fusion.18
  88.8 1.2 copy.43
  90.0 8.5 %all-to-all-start.3 = ((bf16[128,4,512]{2,1,0:T(4,128)(2,1)}), bf16[128,4,512]{2,1,0:T(4,128)(2,1)S(1)}, u32[]{:S(2)}, u32[]{:S(2)}) async-start(bf16[128,4,512]{2,1,0:T(4,128)(2,1)} %copy.43), calls=%async_computation.3 | async-start | bytes 1048576 | tf_op jit(solution)/shard_map/all_to_all | solution.py:82
  98.8 1.3 copy.46
  100.1 2.4 copy.45
  102.6 10.1 %all-to-all-done.3 = bf16[128,4,512]{2,1,0:T(4,128)(2,1)S(1)} async-done(((bf16[128,4,512]{2,1,0:T(4,128)(2,1)}), bf16[128,4,512]{2,1,0:T(4,128)(2,1)S(1)}, u32[]{:S(2)}, u32[]{:S(2)}) %all-to-all-start.3) | async-done | bytes 524320 | tf_op jit(solution)/shard_map/all_to_all | solution.py:82
  113.9 2.0 fusion.10
  119.1 2.8 %convolution_convert_fusion = bf16[4,128,512]{2,1,0:T(8,128)(2,1)} fusion(bf16[1024,512]{1,0:T(8,128)(2,1)} %param.18, bf16[4,128,1024]{2,1,0:T(8,128)(2,1)S(1)} %get-tuple-element.16, f32[4,128]{1,0:T(4,128)S(1)} %add_rsqrt_fusion), kind=kOutput, calls=%fused_computation.27 | convolution fusion | flops 538705920 | bytes 2623488 | tf_op jit(solution)/shard_map/dot_general | solution.py:17
  121.9 59.9 %all-gather.3.cloned.1.call-done = bf16[4,1024,512]{1,2,0:T(8,128)(2,1)} async-done(((bf16[4,128,512]{1,2,0:T(8,128)(2,1)}), bf16[4,1024,512]{1,2,0:T(8,128)(2,1)}) %all-gather.3.cloned.1.call-update) | async-done | bytes 4194320 | tf_op jit(solution)/shard_map/all_gather | solution.py:95
  181.8 4.7 %multiply_reduce_fusion = (f32[4,8,128]{2,1,0:T(8,128)S(1)}, f32[4,8,128,1024]{3,2,1,0:T(8,128)S(1)}) fusion(bf16[4,1024,8,64]{1,3,2,0:T(8,128)(2,1)} %bitcast.77, bf16[4,128,8,32]{1,3,2,0:T(8,128)(2,1)S(1)} %get-tuple-element.6, bf16[4,128,8,32]{1,3,2,0:T(8,128)(2,1)S(1)} %get-tuple-element.5), kind=kOutput, calls=%fused_computation.2 | convolution fusion | flops 546304000 | bytes 21512192 | tf_op jit(solution)/shard_map/sqhd,skhd->shqk/dot_general | solution.py:101
  186.5 5.7 %copy-done.1 = f32[4,8,128,1024]{3,2,1,0:T(8,128)} copy-done((f32[4,8,128,1024]{3,2,1,0:T(8,128)}, f32[4,8,128,1024]{3,2,1,0:T(8,128)S(1)}, u32[]{:S(2)}) %copy-start.1) | copy-done | bytes 16777240
  192.2 3.6 %fusion.1 = f32[4,8,128]{2,1,0:T(8,128)S(1)} fusion(f32[4,8,128,1024]{3,2,1,0:T(8,128)S(1)} %get-tuple-element.18, f32[4,8,128]{2,1,0:T(8,128)S(1)} %broadcast_maximum_fusion), kind=kLoop, calls=%fused_computation.3 | loop fusion | flops 12578816 | bytes 16809984 | tf_op jit(solution)/shard_map/reduce_sum | solution.py:105
  195.8 42.8 %all-gather.5.cloned.1.call-done = bf16[4,1024,512]{2,1,0:T(8,128)(2,1)} async-done(((bf16[4,128,512]{2,1,0:T(8,128)(2,1)}), bf16[4,1024,512]{2,1,0:T(8,128)(2,1)}) %all-gather.5.cloned.1.call-update) | async-done | bytes 4194320 | tf_op jit(solution)/shard_map/all_gather | solution.py:96
  238.6 6.3 %copy.47 = bf16[4,1024,512]{1,2,0:T(8,128)(2,1)} copy(bf16[4,1024,512]{2,1,0:T(8,128)(2,1)} %all-gather.5.cloned.1.call-done) | data formatting | bytes 8388608 | tf_op jit(solution)/shard_map/all_gather | solution.py:96
  245.0 11.1 %divide_convert_fusion = bf16[4,128,8,64]{1,3,2,0:T(8,128)(2,1)} fusion(bf16[4,1024,8,64]{1,3,2,0:T(8,128)(2,1)} %bitcast.76, f32[4,8,128,1024]{3,2,1,0:T(8,128)} %copy-done.1, f32[4,8,128]{2,1,0:T(8,128)S(1)} %broadcast_maximum_fusion, f32[4,128,8]{1,2,0:T(8,128)S(1)} %bitcast.90), kind=kOutput, calls=%fused_computation.45 | convolution fusion | flops 549978112 | bytes 21528576 | tf_op jit(solution)/shard_map/shqk,skhd->shqd/dot_general | solution.py:106
  256.1 2.7 %fusion.12 = bf16[4,128,1024]{2,1,0:T(8,128)(2,1)} fusion(bf16[4,128,1024]{2,1,0:T(8,128)(2,1)S(1)} %get-tuple-element.16, bf16[4,128,512]{1,2,0:T(8,128)(2,1)} %bitcast.88, bf16[512,1024]{1,0:T(8,128)(2,1)S(1)} %copy-done.2), kind=kOutput, calls=%fused_computation.19 | convolution fusion | flops 538443776 | bytes 3670016 | tf_op jit(solution)/shard_map/dot_general | solution.py:17
  (42 shorter events, 6.8 us)
Async XLA Ops:
  6.5 107.3 %copy-start = (bf16[512,1024]{1,0:T(8,128)(2,1)S(1)}, bf16[512,1024]{1,0:T(8,128)(2,1)}, u32[]{:S(2)}) copy-start(bf16[512,1024]{1,0:T(8,128)(2,1)} %param.15) | copy-start | bytes 3145732
  8.1 13.4 %copy-start.6 = (bf16[4,128,1024]{2,1,0:T(8,128)(2,1)S(1)}, bf16[4,128,1024]{2,1,0:T(8,128)(2,1)}, u32[]{:S(2)}) copy-start(bf16[4,128,1024]{2,1,0:T(8,128)(2,1)} %param.10) | copy-start | bytes 3145732
  11.7 24.3 %all-to-all-start.1 = ((bf16[4,128,512]{2,0,1:T(4,128)(2,1)}), bf16[4,128,512]{2,0,1:T(4,128)(2,1)S(1)}, u32[]{:S(2)}, u32[]{:S(2)}) async-start(bf16[4,128,512]{2,0,1:T(4,128)(2,1)} %copy.35), calls=%async_computation.1 | async-start | bytes 1048576 | tf_op jit(solution)/shard_map/all_to_all | solution.py:77
  36.1 22.9 %all-to-all-start.2 = ((bf16[4,128,512]{2,0,1:T(4,128)(2,1)}), bf16[4,128,512]{2,0,1:T(4,128)(2,1)S(1)}, u32[]{:S(2)}, u32[]{:S(2)}) async-start(bf16[4,128,512]{2,0,1:T(4,128)(2,1)} %copy.37), calls=%async_computation.2 | async-start | bytes 1048576 | tf_op jit(solution)/shard_map/all_to_all | solution.py:78
  44.1 23.1 %copy-start.10 = (s32[128]{0:T(128)S(1)}, s32[128]{0:T(128)}, u32[]{:S(2)}) copy-start(s32[128]{0:T(128)} %param.11) | copy-start | bytes 1540
  59.0 22.5 %all-to-all-start = ((bf16[4,128,512]{2,0,1:T(4,128)(2,1)}), bf16[4,128,512]{2,0,1:T(4,128)(2,1)S(1)}, u32[]{:S(2)}, u32[]{:S(2)}) async-start(bf16[4,128,512]{2,0,1:T(4,128)(2,1)} %copy.33), calls=%async_computation | async-start | bytes 1048576 | tf_op jit(solution)/shard_map/all_to_all | solution.py:79
  69.3 13.9 %copy-start.3 = (bf16[128,4,8,64]{3,2,1,0:T(8,128)(2,1)S(1)}, bf16[128,4,8,64]{3,2,1,0:T(8,128)(2,1)}, u32[]{:S(2)}) copy-start(bf16[128,4,8,64]{3,2,1,0:T(8,128)(2,1)} %reshape.173) | copy-start | bytes 1572868
  83.3 3.7 %copy-start.4 = (bf16[128,4,8,64]{3,2,1,0:T(8,128)(2,1)S(1)}, bf16[128,4,8,64]{3,2,1,0:T(8,128)(2,1)}, u32[]{:S(2)}) copy-start(bf16[128,4,8,64]{3,2,1,0:T(8,128)(2,1)} %reshape.172) | copy-start | bytes 1572868
  88.8 10.0 %copy-start.5 = (bf16[1024,512]{1,0:T(8,128)(2,1)S(1)}, bf16[1024,512]{1,0:T(8,128)(2,1)}, u32[]{:S(2)}) copy-start(bf16[1024,512]{1,0:T(8,128)(2,1)} %param.17) | copy-start | bytes 3145732
  90.0 22.7 %all-to-all-start.3 = ((bf16[128,4,512]{2,1,0:T(4,128)(2,1)}), bf16[128,4,512]{2,1,0:T(4,128)(2,1)S(1)}, u32[]{:S(2)}, u32[]{:S(2)}) async-start(bf16[128,4,512]{2,1,0:T(4,128)(2,1)} %copy.43), calls=%async_computation.3 | async-start | bytes 1048576 | tf_op jit(solution)/shard_map/all_to_all | solution.py:82
  98.5 83.3 %all-gather.3.cloned.1.call-start = ((), (), s32[]{:S(2)}) async-start(), calls=%async_computation.4 | async-start | bytes 4718592 | tf_op jit(solution)/shard_map/all_gather | solution.py:95
  100.1 13.8 %copy-start.7 = (bf16[4,128,1024]{2,1,0:T(8,128)(2,1)S(1)}, bf16[4,128,1024]{2,1,0:T(8,128)(2,1)}, u32[]{:S(2)}) copy-start(bf16[4,128,1024]{2,1,0:T(8,128)(2,1)} %param.10) | copy-start | bytes 3145732
  113.9 2.0 copy-start.9
  115.8 1.2 copy-start.8
  119.1 119.6 %all-gather.5.cloned.1.call-start = ((), (), s32[]{:S(2)}) async-start(), calls=%async_computation.5 | async-start | bytes 4718592 | tf_op jit(solution)/shard_map/all_gather | solution.py:96
  186.5 5.7 %copy-start.1 = (f32[4,8,128,1024]{3,2,1,0:T(8,128)}, f32[4,8,128,1024]{3,2,1,0:T(8,128)S(1)}, u32[]{:S(2)}) copy-start(f32[4,8,128,1024]{3,2,1,0:T(8,128)S(1)} %get-tuple-element.18) | copy-start | bytes 50331652
  245.0 11.1 %copy-start.2 = (bf16[512,1024]{1,0:T(8,128)(2,1)S(1)}, bf16[512,1024]{1,0:T(8,128)(2,1)}, u32[]{:S(2)}) copy-start(bf16[512,1024]{1,0:T(8,128)(2,1)} %param.19) | copy-start | bytes 3145732
Sparse Core Ops, SparseCore 0:
  119.2 62.5 all-gather.2
  183.6 54.9 all-gather.4
where the time goes:
time: 270 us; the launch traced here: 266 us
  waiting for transfers between devices  147 us (54%)
  matrix products  36.7 us (14%)
  starting transfers between devices  34.8 us (13%)
  local copies, waits for them, and re-layouts  27.3 us (10%)
  between operations  13.6 us (5%)
  other arithmetic  6.56 us (2%)
    all_gather x1, waiting for transfers between devices, on_device(): key_part = lax.all_gather(key_flat, 'tm', axis=1, tiled=True)  59.9 us
    all_gather x1, waiting for transfers between devices, on_device(): value_part = lax.all_gather(value_t, 'tm', axis=1, tiled=True)  42.8 us
    dot_general x8, matrix products, project(): jnp.dot(normed.reshape(-1, normed.shape[-1]), weight, preferred_element_t...  15.5 us
    all_to_all x1, waiting for transfers between devices, on_device(): lax.all_to_all(key_g, 'series', split_axis=1, concat_axis=0, tiled=True)  11.7 us
    all_to_all x1, waiting for transfers between devices, on_device(): lax.all_to_all(query_g, 'series', split_axis=1, concat_axis=0, tiled=True)  11.3 us
    dot_general x1, matrix products, on_device(): jnp.einsum('shqk,skhd->shqd', weights.astype(jnp.bfloat16), value_h, pref...  11.1 us
    all_to_all x1, waiting for transfers between devices, on_device(): lax.all_to_all(value_g, 'series', split_axis=1, concat_axis=0, tiled=True)  10.7 us
    all_to_all x1, waiting for transfers between devices, on_device(): lax.all_to_all(mixed_r, 'series', split_axis=0, concat_axis=1, tiled=True)  10.1 us
  transfers between devices with their start and end apart: 6, of which 6 were waited for; matrix products, arithmetic and copies ran while one was open for 9% of the time, Pallas kernels for 0%

commit v1 on v0

v1 whole, which is shorter than its diff:
```python
import functools

import jax
import jax.numpy as jnp
from jax import lax
from jax.experimental import pallas as pl
from jax.experimental.pallas import tpu as pltpu
from jax.sharding import Mesh, PartitionSpec as P

HEADS = 8
HEAD_DIM = 64
REACH = 3
BF16 = jnp.bfloat16
F32 = jnp.float32
SERIES = ("zh", "x", "core")
TIME = ("zl", "y")
VMEM_LIMIT = 48 * 1024 * 1024
VMEM = pl.BlockSpec(memory_space=pltpu.VMEM)
ANY = pl.BlockSpec(memory_space=pl.ANY)
SMEM = pl.BlockSpec(memory_space=pltpu.SMEM)


def dot(a, b):
    return jnp.dot(a, b, preferred_element_type=F32)


def normed(values):
    wide = values.astype(F32)
    return (wide * lax.rsqrt(jnp.mean(wide * wide, axis=-1, keepdims=True) + 1e-06)).astype(BF16)


def own_kernel(x_ref, b_ref, wq_ref, wk_ref, wv_ref, q_ref, k_ref, v_ref, kb_ref, vb_ref):
    rows = x_ref.shape[0]
    for at in range(0, rows, 256):
        part = pl.ds(at, 256)
        norm = normed(x_ref[part])
        q_ref[part] = (dot(norm, wq_ref[...]) * HEAD_DIM ** -0.5).astype(BF16)
        k_ref[part] = dot(norm, wk_ref[...]).astype(BF16)
        v_ref[part] = dot(norm, wv_ref[...]).astype(BF16)
    norm = normed(b_ref[...])
    kb_ref[...] = dot(norm, wk_ref[...]).astype(BF16)
    vb_ref[...] = dot(norm, wv_ref[...]).astype(BF16)


def turn(values, cosine, sine):
    lane = lax.broadcasted_iota(jnp.int32, cosine.shape, 1)
    low = lane % HEAD_DIM < HEAD_DIM // 2
    out = []
    for at in range(0, values.shape[1], 128):
        v = values[:, at : at + 128]
        swapped = jnp.where(low, pltpu.roll(v, 96, 1), pltpu.roll(v, 32, 1))
        out.append(v * cosine + swapped * sine)
    return jnp.concatenate(out, axis=1)


def middle_kernel(
    info_ref, x_hbm, q_hbm, k_hbm, v_hbm, kb_hbm, vb_hbm, ha_hbm, wk_hbm, wv_hbm, wo_hbm,
    tq_hbm, tk_hbm, tv_hbm, cos_ref, sin_ref,
    mid_ref, send_ref,
    x_ref, q_ref, kbuf, vbuf, ha_ref, wk_ref, wv_ref, wo_ref, tq_ref, tk_ref, tv_ref, mix_ref, sems,
):
    pt = cos_ref.shape[0]
    base_a = pl.multiple_of(info_ref[0] * pt, pt)
    base_b = pl.multiple_of(info_ref[1] * pt, pt)
    halo = REACH * pt
    own = x_ref.shape[0]
    pairs = [
        (ha_hbm, ha_ref), (wk_hbm, wk_ref), (wv_hbm, wv_ref),
        (k_hbm, kbuf.at[pl.ds(halo, own)]), (kb_hbm, kbuf.at[pl.ds(base_b, halo)]),
        (v_hbm, vbuf.at[pl.ds(halo, own)]), (vb_hbm, vbuf.at[pl.ds(base_b, halo)]),
        (q_hbm, q_ref), (x_hbm, x_ref), (wo_hbm, wo_ref),
        (tq_hbm, tq_ref), (tk_hbm, tk_ref), (tv_hbm, tv_ref),
    ]
    copies = [pltpu.make_async_copy(a, b, sems.at[i]) for i, (a, b) in enumerate(pairs)]
    for c in copies:
        c.start()
    inner = q_ref.shape[1]
    for c in copies[:3]:
        c.wait()
    norm = normed(ha_ref[...])
    kbuf[pl.ds(base_a, halo)] = dot(norm, wk_ref[...]).astype(BF16)
    vbuf[pl.ds(base_a, halo)] = dot(norm, wv_ref[...]).astype(BF16)
    for c in copies[3:8]:
        c.wait()
    row = lax.broadcasted_iota(jnp.int32, (inner, 128), 0)
    col = lax.broadcasted_iota(jnp.int32, (inner, 128), 1)
    gather = (row // HEAD_DIM == col).astype(BF16)
    row = lax.broadcasted_iota(jnp.int32, (128, inner), 0)
    col = lax.broadcasted_iota(jnp.int32, (128, inner), 1)
    spread = (col // HEAD_DIM == row).astype(BF16)
    span = 2 * REACH + 1
    for s in range(own // pt):
        q = q_ref[s * pt : (s + 1) * pt]
        prods = [q * kbuf[(s + j) * pt : (s + j + 1) * pt] for j in range(span)]
        scores = dot(jnp.concatenate(prods, axis=0), gather)
        mine = info_ref[2 + s + REACH]
        parts = []
        for j in range(span):
            same = info_ref[2 + s + j] == mine
            parts.append(jnp.where(same, scores[j * pt : (j + 1) * pt], -1e30))
        top = functools.reduce(jnp.maximum, parts)
        weights = [jnp.exp(p - top) for p in parts]
        inverse = 1.0 / functools.reduce(jnp.add, weights)
        high = inverse.astype(BF16)
        rest = (inverse - high.astype(F32)).astype(BF16)
        wide = dot(jnp.concatenate([w.astype(BF16) for w in weights] + [high, rest], axis=0), spread)
        total = jnp.zeros((pt, inner), F32)
        for j in range(span):
            total += wide[j * pt : (j + 1) * pt] * vbuf[(s + j) * pt : (s + j + 1) * pt].astype(F32)
        total *= wide[span * pt : (span + 1) * pt] + wide[(span + 1) * pt :]
        mix_ref[s * pt : (s + 1) * pt] = total.astype(BF16)
    for c in copies[8:]:
        c.wait()
    cosine, sine = cos_ref[...], sin_ref[...]
    half = inner // 2
    step = 2 * pt
    cosine = jnp.concatenate([cosine, cosine], axis=0)
    sine = jnp.concatenate([sine, sine], axis=0)
    for at in range(0, own, step):
        part = pl.ds(at, step)
        mid = (x_ref[part].astype(F32) + dot(mix_ref[part], wo_ref[...])).astype(BF16)
        mid_ref[part] = mid
        norm = normed(mid)
        q = (turn(dot(norm, tq_ref[...]), cosine, sine) * HEAD_DIM ** -0.5).astype(BF16)
        k = turn(dot(norm, tk_ref[...]), cosine, sine).astype(BF16)
        v = dot(norm, tv_ref[...]).astype(BF16)
        for i in range(2):
            s = at // pt + i
            for h in range(2):
                for n, a in enumerate((q, k, v)):
                    send_ref[2 * s + h, :, n * half : (n + 1) * half] = a[
                        i * pt : (i + 1) * pt, h * half : (h + 1) * half
                    ]


def time_kernel(in_ref, out_ref):
    blocks, pt, width = in_ref.shape
    half = width // 3
    k = in_ref[:, :, half : 2 * half].reshape(blocks * pt, half)
    v = in_ref[:, :, 2 * half :].reshape(blocks * pt, half)
    lane = lax.broadcasted_iota(jnp.int32, (1, half), 1)
    step = 2
    for at in range(0, blocks, step):
        q = in_ref[at : at + step, :, :half].reshape(step * pt, half)
        out = jnp.zeros((step * pt, half), F32)
        for h in range(half // HEAD_DIM):
            keep = lane // HEAD_DIM == h
            scores = lax.dot_general(
                jnp.where(keep, q, jnp.zeros_like(q)), k, (((1,), (1,)), ((), ())),
                preferred_element_type=F32,
            )
            weights = jnp.exp(scores - jnp.max(scores, axis=-1, keepdims=True))
            total = jnp.sum(weights, axis=-1, keepdims=True)
            out = jnp.where(keep, dot(weights.astype(BF16), v) / total, out)
        out_ref[at : at + step] = out.reshape(step, pt, half).astype(BF16)


def out_kernel(mixed_ref, mid_ref, wo_ref, out_ref):
    blocks, pt, half = mixed_ref.shape
    for s in range(blocks // 2):
        part = pl.ds(s * pt, pt)
        mixed = jnp.concatenate([mixed_ref[2 * s], mixed_ref[2 * s + 1]], axis=1)
        out_ref[part] = (mid_ref[part].astype(F32) + dot(mixed, wo_ref[...])).astype(BF16)


def params():
    return pltpu.CompilerParams(vmem_limit_bytes=VMEM_LIMIT)


def cost(flops, moved):
    return pl.CostEstimate(flops=flops, bytes_accessed=moved, transcendentals=0)


def shape(*dims):
    return jax.ShapeDtypeStruct(dims, BF16)


def on_device(
    series_data, group_ids, group_query, group_key, group_value, group_out,
    time_query, time_key, time_value, time_out,
):
    s_dev, pt, feature = series_data.shape
    inner = group_query.shape[1]
    rows, halo = s_dev * pt, REACH * pt
    core = lax.axis_index("core")
    place = lax.axis_index(SERIES)
    count = lax.axis_size(SERIES)
    shift = s_dev - REACH
    x = series_data.reshape(rows, feature)
    to_pair = lax.dynamic_slice_in_dim(x, jnp.where(core == 0, shift * pt, 0), halo)
    to_far = lax.dynamic_slice_in_dim(x, jnp.where(core == 0, 0, shift * pt), halo)
    far = []
    for i in range(1, count - 1, 2):
        far += [(i, i + 1), (i + 1, i)]
    halo_a = lax.ppermute(to_far, SERIES, far)
    halo_b = lax.ppermute(to_pair, "core", [(0, 1), (1, 0)])

    positions = lax.axis_index(TIME) * pt + jnp.arange(pt, dtype=jnp.int32)
    halfway = HEAD_DIM // 2
    freqs = 10000.0 ** (-jnp.arange(halfway, dtype=F32) / halfway)
    angles = positions.astype(F32)[:, None] * freqs[None, :]
    cosine, sine = jnp.cos(angles), jnp.sin(angles)
    cosine = jnp.concatenate([cosine] * 4, axis=1)
    sine = jnp.concatenate([-sine, sine, -sine, sine], axis=1)
    padded = jnp.pad(group_ids, (REACH, REACH), constant_values=-1)
    window = lax.dynamic_slice_in_dim(padded, place * s_dev, s_dev + 2 * REACH)
    right = s_dev + REACH
    base = jnp.stack([jnp.where(core == 0, 0, right), jnp.where(core == 0, right, 0)])
    info = jnp.concatenate([base.astype(jnp.int32), window])

    q, k, v, kb, vb = pl.pallas_call(
        own_kernel,
        out_shape=[shape(rows, inner)] * 3 + [shape(halo, inner)] * 2,
        in_specs=[VMEM] * 5,
        out_specs=[VMEM] * 5,
        compiler_params=params(),
        cost_estimate=cost(2 * feature * inner * (3 * rows + 2 * halo), 8 << 20),
        name="own",
    )(x, halo_b, group_query, group_key, group_value)

    mid, send = pl.pallas_call(
        middle_kernel,
        out_shape=[shape(rows, feature), shape(2 * s_dev, pt, 3 * inner // 2)],
        in_specs=[SMEM] + [ANY] * 13 + [VMEM] * 2,
        out_specs=[VMEM] * 2,
        scratch_shapes=[
            pltpu.VMEM((rows, feature), BF16),
            pltpu.VMEM((rows, inner), BF16),
            pltpu.VMEM((rows + 2 * halo, inner), BF16),
            pltpu.VMEM((rows + 2 * halo, inner), BF16),
            pltpu.VMEM((halo, feature), BF16),
            pltpu.VMEM((feature, inner), BF16),
            pltpu.VMEM((feature, inner), BF16),
            pltpu.VMEM((inner, feature), BF16),
            pltpu.VMEM((feature, inner), BF16),
            pltpu.VMEM((feature, inner), BF16),
            pltpu.VMEM((feature, inner), BF16),
            pltpu.VMEM((rows, inner), BF16),
            pltpu.SemaphoreType.DMA((13,)),
        ],
        compiler_params=params(),
        cost_estimate=cost(2 * feature * inner * (5 * rows + 2 * halo), 14 << 20),
        name="middle",
    )(info, x, q, k, v, kb, vb, halo_a, group_key, group_value, group_out,
      time_query, time_key, time_value, cosine, sine)

    got = lax.all_to_all(send, TIME, split_axis=0, concat_axis=0, tiled=True)
    mixed = pl.pallas_call(
        time_kernel,
        out_shape=shape(2 * s_dev, pt, inner // 2),
        in_specs=[VMEM],
        out_specs=VMEM,
        compiler_params=params(),
        cost_estimate=cost(8 << 30, 2 << 20),
        name="time",
    )(got)
    back = lax.all_to_all(mixed, TIME, split_axis=0, concat_axis=0, tiled=True)
    out = pl.pallas_call(
        out_kernel,
        out_shape=shape(rows, feature),
        in_specs=[VMEM] * 3,
        out_specs=VMEM,
        compiler_params=params(),
        cost_estimate=cost(2 * feature * inner * rows, 4 << 20),
        name="out",
    )(back, mid, time_out)
    return out.reshape(s_dev, pt, feature)


def solution(mesh):
    names = ("zh", "x", "core", "zl", "y")
    fine = Mesh(mesh.devices.reshape(4, 4, 2, 2, 4), names)
    whole = P(SERIES, TIME, None)
    placed = (whole,) + (P(),) * 9
    return jax.shard_map(
        on_device, mesh=fine, in_specs=placed, out_specs=whole, check_vma=False
    )
```

time: 270 us -> 78.4 us (0.29); the launches traced: 266 us -> 78.1 us
  waiting for transfers between devices: 147 us -> 17.3 us
  matrix products: 36.7 us -> 0 us
  starting transfers between devices: 34.8 us -> 3.59 us
  blocking collectives: 0 us -> 30.9 us
  local copies, waits for them, and re-layouts: 27.3 us -> 2.88 us
  Pallas kernels: 0 us -> 22.7 us
  between operations: 13.6 us -> 0.07 us
  other arithmetic: 6.56 us -> 0.57 us
    all_gather x2 -> x0, waiting for transfers between devices: 103 us -> none  [the longest x1 59.9 us: on_device(): key_part = lax.all_gather(key_flat, 'tm', axis=1, tiled=True)]
    all_to_all x4 -> x0, waiting for transfers between devices: 43.9 us -> none  [the longest x1 11.7 us: on_device(): lax.all_to_all(key_g, 'series', split_axis=1, concat_axis=0, tiled=True)]
    all_to_all x4 -> x0, starting transfers between devices: 34.6 us -> none  [the longest x1 9.82 us: on_device(): lax.all_to_all(query_g, 'series', split_axis=1, concat_axis=0, tiled=True)]
    dot_general x11 -> x0, matrix products: 33 us -> none  [the longest x8 15.5 us: project(): jnp.dot(normed.reshape(-1, normed.shape[-1]), weight, preferred_element_t...]
    all_to_all x0 -> x2, blocking collectives: none -> 30.9 us  [the longest x1 18.8 us: on_device(): got = lax.all_to_all(send, TIME, split_axis=0, concat_axis=0, tiled=True)]
    pallas_call x0 -> x4, Pallas kernels: none -> 22.7 us  [the longest x1 10.8 us: on_device(): pl.pallas_call(middle_kernel, out_shape=[shape(rows, feature), shape(2 *...]
    ppermute x0 -> x2, waiting for transfers between devices: none -> 17.3 us  [the longest x1 15.7 us: on_device(): halo_a = lax.ppermute(to_far, SERIES, far)]
    unnamed x24 -> x8, local copies, waits for them, and re-layouts: 9.81 us -> 0.02 us
  transfers between devices with their start and end apart: 6 -> 2, of which waited for: 6 -> 2; matrix products, arithmetic and copies ran while one was open for 9% -> 1% of each run, Pallas kernels for 0% -> 6%
where the time goes in v1:
time: 78.4 us; the launch traced here: 78.1 us
  blocking collectives  30.9 us (39%)
  Pallas kernels  22.7 us (29%)
  waiting for transfers between devices  17.3 us (22%)
  starting transfers between devices  3.59 us (5%)
  local copies, waits for them, and re-layouts  2.88 us (4%)
    all_to_all x1, blocking collectives, on_device(): got = lax.all_to_all(send, TIME, split_axis=0, concat_axis=0, tiled=True)  18.8 us
    ppermute x1, waiting for transfers between devices, on_device(): halo_a = lax.ppermute(to_far, SERIES, far)  15.7 us
    all_to_all x1, blocking collectives, on_device(): back = lax.all_to_all(mixed, TIME, split_axis=0, concat_axis=0, tiled=True)  12.1 us
    pallas_call x1, Pallas kernels, on_device(): pl.pallas_call(middle_kernel, out_shape=[shape(rows, feature), shape(2 *...  10.8 us
    pallas_call x1, Pallas kernels, on_device(): pl.pallas_call(time_kernel, out_shape=shape(2 * s_dev, pt, inner // 2), i...  5.76 us
    pallas_call x1, Pallas kernels, on_device(): pl.pallas_call(own_kernel, out_shape=[shape(rows, inner)] * 3 + [shape(ha...  4.48 us
    ppermute x1, starting transfers between devices, on_device(): halo_a = lax.ppermute(to_far, SERIES, far)  3.18 us
    dynamic_slice x1, local copies, waits for them, and re-layouts, on_device(): lax.dynamic_slice_in_dim(x, jnp.where(core == 0, 0, shift * pt), halo)  2.78 us
  transfers between devices with their start and end apart: 2, of which 2 were waited for; matrix products, arithmetic and copies ran while one was open for 1% of the time, Pallas kernels for 6%

profile of v1, /device:TPU:128, one launch (start us, length us, event | category | flops | bytes accessed | tf_op | source)
XLA Modules:
  0.0 78.1 jit_solution(8185483100226319739)
XLA Ops:
  0.0 0.0 copy-start.3
  0.0 0.0 copy-start
  0.0 0.0 copy-start.2
  0.0 2.8 %constant_dynamic-slice_fusion = (bf16[384,1024]{1,0:T(8,128)(2,1)}, bf16[384,1024]{1,0:T(8,128)(2,1)}) fusion(bf16[512,1024]{1,0:T(8,128)(2,1)} %bitcast.4, s32[]{:T(128)S(6)} %select_n.22, s32[]{:T(128)S(6)} %select_n.21), kind=kLoop, calls=%fused_computation.9 | loop fusion | bytes 3145736 | tf_op jit(solution)/shard_map/dynamic_slice | solution.py:191
  2.8 3.2 %collective-permute-start.1 = (bf16[384,1024]{1,0:T(8,128)(2,1)}, bf16[384,1024]{1,0:T(8,128)(2,1)S(1)}, u32[]{:S(2)}, u32[]{:S(2)}) collective-permute-start(bf16[384,1024]{1,0:T(8,128)(2,1)} %get-tuple-element.19), channel_id=1, source_target_pairs={{8,16},{16,8},{24,32},{32,24},{40,48},{48,40},{56,64},{64,56},{72,... | collective-permute-start | bytes 2359304 | tf_op jit(solution)/shard_map/ppermute | solution.py:195
  6.0 0.4 collective-permute-start
  6.4 0.0 copy-done.3
  6.4 0.1 pad_dynamic-slice_fusion
  6.5 0.1 pad_add_fusion.info_ref
  6.6 0.3 fusion
  6.9 0.2 pad_maximum_fusion
  7.1 1.6 %collective-permute-done.b_ref = bf16[384,1024]{1,0:T(8,128)(2,1)} collective-permute-done((bf16[384,1024]{1,0:T(8,128)(2,1)}, bf16[384,1024]{1,0:T(8,128)(2,1)}, u32[]{:S(2)}, u32[]{:S(2)}) %collective-permute-start) | collective-permute-done | bytes 786464 | tf_op jit(solution)/shard_map/ppermute | solution.py:196
  8.7 0.0 copy-done
  8.7 0.0 copy-done.2
  8.7 4.5 %own.1 = (bf16[512,512]{1,0:T(8,128)(2,1)S(1)}, bf16[512,512]{1,0:T(8,128)(2,1)S(1)}, bf16[512,512]{1,0:T(8,128)(2,1)S(1)}, bf16[384,512]{1,0:T(8,128)(2,1)S(1)}, bf16[384,512]{1,0:T(8,128)(2,1)S(1)}) custom-call(bf16[512,1024]{1,0:T(8,128)(2,1)S(1)} %bitcast.5, bf16[384,1024]{1,0:T(8,128)(2,1)} %collective-permute-done.b_ref, ...), custom_call_target="tpu_custom_call" | custom-call | flops 2415919104 | bytes 8388608 | tf_op jit(solution)/shard_map/own/pallas_call | solution.py:211
  13.2 15.7 %collective-permute-done.1.ha_hbm = bf16[384,1024]{1,0:T(8,128)(2,1)S(1)} collective-permute-done((bf16[384,1024]{1,0:T(8,128)(2,1)}, bf16[384,1024]{1,0:T(8,128)(2,1)S(1)}, u32[]{:S(2)}, u32[]{:S(2)}) %collective-permute-start.1) | collective-permute-done | bytes 786464 | tf_op jit(solution)/shard_map/ppermute | solution.py:195
  28.9 10.8 %middle.1 = (bf16[512,1024]{1,0:T(8,128)(2,1)S(1)}, bf16[8,128,768]{2,1,0:T(8,128)(2,1)}) custom-call(s32[12]{0:T(128)S(1)} %pad_add_fusion.info_ref, bf16[512,1024]{1,0:T(8,128)(2,1)S(1)} %bitcast.6, bf16[512,512]{1,0:T(8,128)(2,1)S(1)} %get-tuple-element.12.q_hbm, bf16[512,512]{1,0:T(8,128)(2,1)S(1)} %get-tuple-element.13.k_hbm, ...), custom_call_target="tpu_custom_call" | custom-call | flops 3489660928 | bytes 14680064 | tf_op jit(solution)/shard_map/middle/pallas_call | solution.py:221
  39.7 18.8 %all_to_all.10.in_ref = bf16[8,128,768]{2,1,0:T(8,128)(2,1)S(1)} all-to-all(bf16[8,128,768]{2,1,0:T(8,128)(2,1)} %get-tuple-element.17), channel_id=1, replica_groups=mesh['zh'=4,'x'=4,'core'=2,'zl'=2,'y'=4] {'zl','y'}, dimensions={0} | all-to-all | bytes 3145728 | tf_op jit(solution)/shard_map/all_to_all | solution.py:247
  58.5 5.8 %time.1 = bf16[8,128,256]{2,1,0:T(8,128)(2,1)S(1)} custom-call(bf16[8,128,768]{2,1,0:T(8,128)(2,1)S(1)} %all_to_all.10.in_ref), custom_call_target="tpu_custom_call" | custom-call | flops 8589934592 | bytes 2097152 | tf_op jit(solution)/shard_map/time/pallas_call | solution.py:248
  64.3 0.0 copy-start.1
  64.3 12.1 %all_to_all.11.mixed_ref = bf16[8,128,256]{2,1,0:T(8,128)(2,1)S(1)} all-to-all(bf16[8,128,256]{2,1,0:T(8,128)(2,1)S(1)} %time.1), channel_id=1, replica_groups=mesh['zh'=4,'x'=4,'core'=2,'zl'=2,'y'=4] {'zl','y'}, dimensions={0} | all-to-all | bytes 1048576 | tf_op jit(solution)/shard_map/all_to_all | solution.py:257
  76.4 0.0 copy-done.1
  76.4 1.7 %out.1 = bf16[512,1024]{1,0:T(8,128)(2,1)} custom-call(bf16[8,128,256]{2,1,0:T(8,128)(2,1)S(1)} %all_to_all.11.mixed_ref, bf16[512,1024]{1,0:T(8,128)(2,1)S(1)} %get-tuple-element.18.mid_ref, bf16[512,1024]{1,0:T(8,128)(2,1)S(1)} %copy-done.1), custom_call_target="tpu_custom_call" | custom-call | flops 536870912 | bytes 4194304 | tf_op jit(solution)/shard_map/out/pallas_call | solution.py:258
  (2 shorter events, 0.0 us)
Async XLA Ops:
  0.0 6.4 %copy-start.3 = (s32[128]{0:T(128)S(1)}, s32[128]{0:T(128)}, u32[]{:S(2)}) copy-start(s32[128]{0:T(128)} %param.11) | copy-start | bytes 1540
  0.0 8.7 %copy-start = (bf16[4,128,1024]{2,1,0:T(8,128)(2,1)S(1)}, bf16[4,128,1024]{2,1,0:T(8,128)(2,1)}, u32[]{:S(2)}) copy-start(bf16[4,128,1024]{2,1,0:T(8,128)(2,1)} %param.10) | copy-start | bytes 3145732
  0.0 8.7 %copy-start.2 = (bf16[1024,512]{1,0:T(8,128)(2,1)S(1)}, bf16[1024,512]{1,0:T(8,128)(2,1)}, u32[]{:S(2)}) copy-start(bf16[1024,512]{1,0:T(8,128)(2,1)} %wq_ref.1) | copy-start | bytes 3145732
  2.8 26.1 %collective-permute-start.1 = (bf16[384,1024]{1,0:T(8,128)(2,1)}, bf16[384,1024]{1,0:T(8,128)(2,1)S(1)}, u32[]{:S(2)}, u32[]{:S(2)}) collective-permute-start(bf16[384,1024]{1,0:T(8,128)(2,1)} %get-tuple-element.19), channel_id=1, source_target_pairs={{8,16},{16,8},{24,32},{32,24},{40,48},{48,40},{56,64},{64,56},{72,... | collective-permute-start | bytes 2359304 | tf_op jit(solution)/shard_map/ppermute | solution.py:195
  6.0 2.7 %collective-permute-start = (bf16[384,1024]{1,0:T(8,128)(2,1)}, bf16[384,1024]{1,0:T(8,128)(2,1)}, u32[]{:S(2)}, u32[]{:S(2)}) collective-permute-start(bf16[384,1024]{1,0:T(8,128)(2,1)} %get-tuple-element.20), channel_id=1, source_target_pairs={{0,8},{8,0},{1,9},{9,1},{2,10},{10,2},{3,11},{11,3},{4,12},{12,4},... | collective-permute-start | bytes 2359304 | tf_op jit(solution)/shard_map/ppermute | solution.py:196
  64.3 12.1 %copy-start.1 = (bf16[512,1024]{1,0:T(8,128)(2,1)S(1)}, bf16[512,1024]{1,0:T(8,128)(2,1)}, u32[]{:S(2)}) copy-start(bf16[512,1024]{1,0:T(8,128)(2,1)} %wo_ref.1) | copy-start | bytes 3145732

commit v2 on v1

v2 whole, which is shorter than its diff:
```python
import functools

import jax
import jax.numpy as jnp
from jax import lax
from jax.experimental import pallas as pl
from jax.experimental.pallas import tpu as pltpu
from jax.sharding import Mesh, PartitionSpec as P

HEADS = 8
HEAD_DIM = 64
REACH = 3
BF16 = jnp.bfloat16
F32 = jnp.float32
SERIES = ("zh", "x", "core")
TIME = ("zl", "y")
VMEM = pl.BlockSpec(memory_space=pltpu.VMEM)
ANY = pl.BlockSpec(memory_space=pl.ANY)
HBM = pl.BlockSpec(memory_space=pltpu.HBM)
SMEM = pl.BlockSpec(memory_space=pltpu.SMEM)


def dot(a, b):
    return jnp.dot(a, b, preferred_element_type=F32)


def normed(values):
    wide = values.astype(F32)
    return (wide * lax.rsqrt(jnp.mean(wide * wide, axis=-1, keepdims=True) + 1e-06)).astype(BF16)


def cut_kernel(x_hbm, far_ref, sems):
    rows, halo = x_hbm.shape[0], far_ref.shape[0]
    pt = rows - halo
    first = pl.multiple_of(jnp.where(lax.axis_index("core") == 0, 0, pt), pt)
    step = halo // sems.shape[0]
    copies = [
        pltpu.make_async_copy(
            x_hbm.at[pl.ds(first + i * step, step)], far_ref.at[pl.ds(i * step, step)], sems.at[i]
        )
        for i in range(sems.shape[0])
    ]
    for c in copies:
        c.start()
    for c in copies:
        c.wait()


def head_maps(inner):
    row = lax.broadcasted_iota(jnp.int32, (inner, 128), 0)
    col = lax.broadcasted_iota(jnp.int32, (inner, 128), 1)
    gather = (row // HEAD_DIM == col).astype(BF16)
    row = lax.broadcasted_iota(jnp.int32, (128, inner), 0)
    col = lax.broadcasted_iota(jnp.int32, (128, inner), 1)
    return gather, (col // HEAD_DIM == row).astype(BF16)


def attend(q, keys, values, same, gather, spread):
    pt = q.shape[0]
    scores = dot(jnp.concatenate([q * k for k in keys], axis=0), gather)
    parts = [jnp.where(m, scores[j * pt : (j + 1) * pt], -1e30) for j, m in enumerate(same)]
    top = functools.reduce(jnp.maximum, parts)
    weights = [jnp.exp(p - top) for p in parts]
    inverse = 1.0 / functools.reduce(jnp.add, weights)
    high = inverse.astype(BF16)
    low = (inverse - high.astype(F32)).astype(BF16)
    wide = dot(jnp.concatenate([w.astype(BF16) for w in weights] + [high, low], axis=0), spread)
    total = jnp.zeros(q.shape, F32)
    for j, v in enumerate(values):
        total += wide[j * pt : (j + 1) * pt] * v.astype(F32)
    last = len(keys) * pt
    return (total * (wide[last : last + pt] + wide[last + pt :])).astype(BF16)


def turn(values, cosine, sine):
    lane = lax.broadcasted_iota(jnp.int32, cosine.shape, 1)
    low = lane % HEAD_DIM < HEAD_DIM // 2
    out = []
    for at in range(0, values.shape[1], 128):
        v = values[:, at : at + 128]
        swapped = jnp.where(low, pltpu.roll(v, 96, 1), pltpu.roll(v, 32, 1))
        out.append(v * cosine + swapped * sine)
    return jnp.concatenate(out, axis=1)


def advance(x, mixed, wo_ref, tq_ref, tk_ref, tv_ref, cosine, sine):
    mid = (x.astype(F32) + dot(mixed, wo_ref[...])).astype(BF16)
    norm = normed(mid)
    q = (turn(dot(norm, tq_ref[...]), cosine, sine) * HEAD_DIM ** -0.5).astype(BF16)
    k = turn(dot(norm, tk_ref[...]), cosine, sine).astype(BF16)
    return mid, q, k, dot(norm, tv_ref[...]).astype(BF16)


def fetch(sources, targets, sems):
    copies = []
    for i, (a, b) in enumerate(zip(sources, targets)):
        rows = a.shape[0] // 2
        copies.append([
            pltpu.make_async_copy(a.at[pl.ds(n * rows, rows)], b.at[pl.ds(n * rows, rows)], sems.at[i, n])
            for n in range(2)
        ])
    for c in copies:
        c[0].start()
        c[1].start()

    def wait(*which):
        for i in which:
            copies[i][0].wait()
            copies[i][1].wait()

    return wait


def own_kernel(
    ids_ref, x_ref, pair_ref, wq_hbm, wk_hbm, wv_hbm, wo_hbm, tq_hbm, tk_hbm, tv_hbm, cos_ref, sin_ref,
    q_ref, k_ref, v_ref, mid_ref, send_ref, wk_ref, wv_ref, wo_ref, tq_ref, tk_ref, tv_ref,
    mix_ref, wq_ref, sems,
):
    wait = fetch(
        (wq_hbm, wk_hbm, wv_hbm, wo_hbm, tq_hbm, tk_hbm, tv_hbm),
        (wq_ref, wk_ref, wv_ref, wo_ref, tq_ref, tk_ref, tv_ref), sems,
    )
    pt, rows, inner = cos_ref.shape[0], x_ref.shape[0], q_ref.shape[1]
    own, halo = rows // pt, REACH * pt
    first = lax.axis_index("core") == 0
    own_spot = jnp.where(first, 0, REACH)
    pair_row = pl.multiple_of(jnp.where(first, rows, 0), pt)
    own_row = pl.multiple_of(own_spot * pt, pt)
    step = 2 * pt
    wait(0, 1, 2)
    for at in range(0, rows, step):
        norm = normed(x_ref[pl.ds(at, step)])
        part = pl.ds(pl.multiple_of(own_row + at, pt), step)
        q_ref[pl.ds(at, step)] = (dot(norm, wq_ref[...]) * HEAD_DIM ** -0.5).astype(BF16)
        k_ref[part] = dot(norm, wk_ref[...]).astype(BF16)
        v_ref[part] = dot(norm, wv_ref[...]).astype(BF16)
    source = pl.multiple_of(jnp.where(first, 0, pt), pt)
    norm = normed(pair_ref[pl.ds(source, halo)])
    k_ref[pl.ds(pair_row, halo)] = dot(norm, wk_ref[...]).astype(BF16)
    v_ref[pl.ds(pair_row, halo)] = dot(norm, wv_ref[...]).astype(BF16)
    gather, spread = head_maps(inner)
    span, count = REACH + 1, ids_ref.shape[0]
    place = lax.axis_index(SERIES) * own
    for s in range(own):
        index = place + s
        mine = ids_ref[index]
        back = jnp.int32(0)
        for j in range(1, span):
            back += ((ids_ref[jnp.maximum(index - j, 0)] == mine) & (index >= j)).astype(jnp.int32)
        start = jnp.clip(own_spot + s - back, 0, REACH)
        spots = [pl.ds(pl.multiple_of((start + j) * pt, pt), pt) for j in range(span)]
        others = [place - own_spot + start + j for j in range(span)]
        same = [
            (ids_ref[jnp.clip(o, 0, count - 1)] == mine) & (o >= 0) & (o < count) for o in others
        ]
        mix_ref[s * pt : (s + 1) * pt] = attend(
            q_ref[s * pt : (s + 1) * pt], [k_ref[p] for p in spots], [v_ref[p] for p in spots],
            same, gather, spread,
        )
    wait(3, 4, 5, 6)
    half = inner // 2
    cosine = jnp.concatenate([cos_ref[...]] * 2, axis=0)
    sine = jnp.concatenate([sin_ref[...]] * 2, axis=0)
    for at in range(0, rows, step):
        part = pl.ds(at, step)
        mid, q, k, v = advance(x_ref[part], mix_ref[part], wo_ref, tq_ref, tk_ref, tv_ref, cosine, sine)
        mid_ref[part] = mid
        for i in range(2):
            for h in range(2):
                for n, a in enumerate((q, k, v)):
                    send_ref[2 * (at // pt + i) + h, :, n * half : (n + 1) * half] = a[
                        i * pt : (i + 1) * pt, h * half : (h + 1) * half
                    ]


def fix_kernel(
    ids_ref, far_ref, x_ref, q_ref, k_ref, v_ref, wk_ref, wv_ref, wo_ref, tq_ref, tk_ref, tv_ref,
    cos_ref, sin_ref, mid_in, send_in,
    mid_out, send_out,
    fk_ref, fv_ref, mix_ref, mid_ref, send_ref, sems,
):
    del mid_in, send_in
    pt, rows, inner = cos_ref.shape[0], x_ref.shape[0], q_ref.shape[1]
    own, count = rows // pt, ids_ref.shape[0]
    first = lax.axis_index("core") == 0
    place = lax.axis_index(SERIES) * own
    edge = jnp.where(first, place, place + own - 1)
    way = jnp.where(first, -1, 1)
    mine = ids_ref[edge]

    def run(start, step, most):
        size = jnp.int32(0)
        for j in range(most):
            at = start + j * step
            size += ((at >= 0) & (at < count) & (ids_ref[jnp.clip(at, 0, count - 1)] == mine)).astype(jnp.int32)
        return size

    far = run(edge + way, way, REACH)
    near = run(edge, -way, REACH)
    half, halo = inner // 2, REACH * pt
    base = pl.multiple_of(jnp.where(first, 0, pt), pt)
    lows = [pl.multiple_of(jnp.where(first, j, REACH - 1 - j) * pt, pt) for j in range(REACH)]

    def finish(low, size):
        cosine = jnp.concatenate([cos_ref[...]] * (size // pt), axis=0)
        sine = jnp.concatenate([sin_ref[...]] * (size // pt), axis=0)
        x = x_ref[pl.ds(pl.multiple_of(base + low, pt), size)]
        mid, q, k, v = advance(
            x, mix_ref[pl.ds(low, size)], wo_ref, tq_ref, tk_ref, tv_ref, cosine, sine
        )
        mid_ref[pl.ds(low, size)] = mid
        for i in range(size // pt):
            for h in range(2):
                for n, a in enumerate((q, k, v)):
                    send_ref[2 * (low // pt + i) + h, :, n * half : (n + 1) * half] = a[
                        i * pt : (i + 1) * pt, h * half : (h + 1) * half
                    ]

    @pl.when(far > 0)
    def _():
        gather, spread = head_maps(inner)
        own_spot = jnp.where(first, 0, REACH)
        for j in range(REACH):

            @pl.when(j < far)
            def _():
                spot = pl.ds(pl.multiple_of(jnp.where(first, REACH - 1 - j, j) * pt, pt), pt)
                norm = normed(far_ref[spot])
                fk_ref[j * pt : (j + 1) * pt] = dot(norm, wk_ref[...]).astype(BF16)
                fv_ref[j * pt : (j + 1) * pt] = dot(norm, wv_ref[...]).astype(BF16)

        for j in range(REACH):

            @pl.when(j < near)
            def _():
                spots = []
                for i in range(REACH):
                    at = own_spot + jnp.where(first, i, own - 1 - i)
                    spots.append(pl.ds(pl.multiple_of(at * pt, pt), pt))
                two, three = far >= 2, far >= 3
                keys, values = [], []
                for ref, own_ref, into in ((fk_ref, k_ref, keys), (fv_ref, v_ref, values)):
                    into.append(ref[0:pt])
                    into.append(jnp.where(two, ref[pt : 2 * pt], own_ref[spots[2]]))
                    into.append(jnp.where(three, ref[2 * pt : 3 * pt], own_ref[spots[1]]))
                    into.append(own_ref[spots[0]])
                same = [far >= 1, two | (near >= 3), three | (near >= 2), near >= 1]
                q = q_ref[pl.ds(pl.multiple_of(base + lows[j], pt), pt)]
                mix_ref[pl.ds(lows[j], pt)] = attend(q, keys, values, same, gather, spread)

        @pl.when((near == 1) & first)
        def _():
            finish(0, pt)

        @pl.when((near == 1) & jnp.logical_not(first))
        def _():
            finish(halo - pt, pt)

        @pl.when(near > 1)
        def _():
            finish(0, halo)

        def copies(j):
            slot = jnp.where(first, j, own - 1 - j)
            block = jnp.where(first, j, REACH - 1 - j)
            row = pl.ds(pl.multiple_of(slot * pt, pt), pt)
            return (
                pltpu.make_async_copy(mid_ref.at[pl.ds(lows[j], pt)], mid_out.at[row], sems.at[j, 0]),
                pltpu.make_async_copy(
                    send_ref.at[pl.ds(2 * block, 2)], send_out.at[pl.ds(2 * slot, 2)], sems.at[j, 1]
                ),
            )

        for j in range(REACH):

            @pl.when(j < near)
            def _():
                for c in copies(j):
                    c.start()

        for j in range(REACH):

            @pl.when(j < near)
            def _():
                for c in copies(j):
                    c.wait()


def time_kernel(in_ref, out_ref, v_ref):
    blocks, pt, width = in_ref.shape
    half = width // 3
    heads = half // HEAD_DIM
    k = in_ref[:, :, half : 2 * half].reshape(blocks * pt, half)
    v = in_ref[:, :, 2 * half :].reshape(blocks * pt, half)
    keeps = [lax.broadcasted_iota(jnp.int32, (1, half), 1) // HEAD_DIM == h for h in range(heads)]
    for h in range(heads):
        v_ref[h] = jnp.where(keeps[h], v, jnp.ones_like(v))
    step = 2
    for at in range(0, blocks, step):
        q = in_ref[at : at + step, :, :half].reshape(step * pt, half)
        out = jnp.zeros((step * pt, half), F32)
        for h in range(heads):
            scores = lax.dot_general(
                jnp.where(keeps[h], q, jnp.zeros_like(q)), k, (((1,), (1,)), ((), ())),
                preferred_element_type=F32,
            )
            weights = jnp.exp(scores - jnp.max(scores, axis=-1, keepdims=True)).astype(BF16)
            both = dot(weights, v_ref[h])
            out = jnp.where(keeps[h], both / pltpu.roll(both, half // 2, 1), out)
        out_ref[at : at + step] = out.reshape(step, pt, half).astype(BF16)


def out_kernel(mixed_ref, mid_ref, wo_ref, out_hbm, out_ref, sems):
    blocks, pt, half = mixed_ref.shape
    copies = []
    for s in range(blocks // 2):
        part = pl.ds(s * pt, pt)
        mixed = jnp.concatenate([mixed_ref[2 * s], mixed_ref[2 * s + 1]], axis=1)
        out_ref[part] = (mid_ref[part].astype(F32) + dot(mixed, wo_ref[...])).astype(BF16)
        copies.append(pltpu.make_async_copy(out_ref.at[part], out_hbm.at[part], sems.at[s]))
        copies[-1].start()
    for c in copies:
        c.wait()


def params(mib=32):
    return pltpu.CompilerParams(vmem_limit_bytes=mib << 20)


def cost(flops, moved):
    return pl.CostEstimate(flops=flops, bytes_accessed=moved, transcendentals=0)


def shape(*dims):
    return jax.ShapeDtypeStruct(dims, BF16)


def on_device(
    series_data, group_ids, group_query, group_key, group_value, group_out,
    time_query, time_key, time_value, time_out,
):
    s_dev, pt, feature = series_data.shape
    inner = group_query.shape[1]
    rows, halo = s_dev * pt, REACH * pt
    x = series_data.reshape(rows, feature)
    swaps = []
    for i in range(1, lax.axis_size(SERIES) - 1, 2):
        swaps += [(i, i + 1), (i + 1, i)]
    to_far = pl.pallas_call(
        cut_kernel,
        out_shape=shape(halo, feature),
        in_specs=[HBM],
        out_specs=VMEM,
        scratch_shapes=[pltpu.SemaphoreType.DMA((6,))],
        compiler_params=params(62),
        cost_estimate=cost(0, 2 << 20),
        name="cut",
    )(x)
    to_far, x = lax.optimization_barrier((to_far, x))
    far = lax.ppermute(to_far, SERIES, swaps)
    pair = lax.ppermute(x, "core", [(0, 1), (1, 0)])

    positions = lax.axis_index(TIME) * pt + jnp.arange(pt, dtype=jnp.int32)
    halfway = HEAD_DIM // 2
    freqs = 10000.0 ** (-jnp.arange(halfway, dtype=F32) / halfway)
    angles = positions.astype(F32)[:, None] * freqs[None, :]
    cosine, sine = jnp.cos(angles), jnp.sin(angles)
    cosine = jnp.concatenate([cosine] * 4, axis=1)
    sine = jnp.concatenate([-sine, sine, -sine, sine], axis=1)
    weights = (group_query, group_key, group_value, group_out, time_query, time_key, time_value)
    mid_shape, send_shape = shape(rows, feature), shape(2 * s_dev, pt, 3 * inner // 2)
    q, k, v, mid, send, *loaded = pl.pallas_call(
        own_kernel,
        out_shape=[shape(rows, inner)] + [shape(rows + halo, inner)] * 2 + [mid_shape, send_shape]
        + [shape(*w.shape) for w in weights[1:]],
        in_specs=[SMEM] + [VMEM] * 2 + [HBM] * 7 + [VMEM] * 2,
        out_specs=[VMEM] * 11,
        scratch_shapes=[
            pltpu.VMEM((rows, inner), BF16),
            pltpu.VMEM(group_query.shape, BF16),
            pltpu.SemaphoreType.DMA((7, 2)),
        ],
        compiler_params=params(41),
        cost_estimate=cost(2 * feature * inner * (7 * rows + 2 * halo), 16 << 20),
        name="own",
    )(group_ids, x, pair, *weights, cosine, sine)
    mid, send = pl.pallas_call(
        fix_kernel,
        out_shape=[mid_shape, send_shape],
        in_specs=[SMEM] + [VMEM] * 13 + [ANY] * 2,
        out_specs=[ANY] * 2,
        scratch_shapes=[
            pltpu.VMEM((halo, inner), BF16),
            pltpu.VMEM((halo, inner), BF16),
            pltpu.VMEM((halo, inner), BF16),
            pltpu.VMEM((halo, feature), BF16),
            pltpu.VMEM((2 * REACH, pt, 3 * inner // 2), BF16),
        ]
        + [pltpu.SemaphoreType.DMA((REACH, 2))],
        input_output_aliases={14: 0, 15: 1},
        compiler_params=params(),
        cost_estimate=cost(2 * feature * inner * 7 * pt, 4 << 20),
        name="fix",
    )(group_ids, far, x, q, k, v, *loaded, cosine, sine, mid, send)

    got = lax.all_to_all(send, TIME, split_axis=0, concat_axis=0, tiled=True)
    mixed = pl.pallas_call(
        time_kernel,
        out_shape=shape(2 * s_dev, pt, inner // 2),
        in_specs=[VMEM],
        out_specs=VMEM,
        scratch_shapes=[pltpu.VMEM((HEADS // 2, 2 * s_dev * pt, inner // 2), BF16)],
        compiler_params=params(),
        cost_estimate=cost(8 << 30, 2 << 20),
        name="time",
    )(got)
    back = lax.all_to_all(mixed, TIME, split_axis=0, concat_axis=0, tiled=True)
    out = pl.pallas_call(
        out_kernel,
        out_shape=shape(rows, feature),
        in_specs=[VMEM] * 3,
        out_specs=HBM,
        scratch_shapes=[pltpu.VMEM((rows, feature), BF16), pltpu.SemaphoreType.DMA((s_dev,))],
        compiler_params=params(),
        cost_estimate=cost(2 * feature * inner * rows, 4 << 20),
        name="out",
    )(back, mid, time_out)
    return out.reshape(s_dev, pt, feature)


def solution(mesh):
    names = ("zh", "x", "core", "zl", "y")
    fine = Mesh(mesh.devices.reshape(4, 4, 2, 2, 4), names)
    whole = P(SERIES, TIME, None)
    placed = (whole,) + (P(),) * 9
    return jax.shard_map(
        on_device, mesh=fine, in_specs=placed, out_specs=whole, check_vma=False
    )
```

time: 78.4 us -> 73.9 us (0.943)
  the two profiles are of different devices: /device:TPU:128 before, /device:TPU:64 now
where the time goes in v2:
time: 73.9 us; the launch traced here: 73.8 us
  blocking collectives  35 us (47%)
  Pallas kernels  27.3 us (37%)
  waiting for transfers between devices  4.15 us (6%)
  starting transfers between devices  3.94 us (5%)
  local copies, waits for them, and re-layouts  2.64 us (4%)
    all_to_all x1, blocking collectives, on_device(): got = lax.all_to_all(send, TIME, split_axis=0, concat_axis=0, tiled=True)  22.5 us
    all_to_all x1, blocking collectives, on_device(): back = lax.all_to_all(mixed, TIME, split_axis=0, concat_axis=0, tiled=True)  12.5 us
    pallas_call x1, Pallas kernels, on_device(): pl.pallas_call(own_kernel, out_shape=[shape(rows, inner)] + [shape(rows +...  12.3 us
    pallas_call x1, Pallas kernels, on_device(): pl.pallas_call(fix_kernel, out_shape=[mid_shape, send_shape], in_specs=[S...  5.95 us
    pallas_call x1, Pallas kernels, on_device(): pl.pallas_call(time_kernel, out_shape=shape(2 * s_dev, pt, inner // 2), i...  5.37 us
    ppermute x1, waiting for transfers between devices, on_device(): far = lax.ppermute(to_far, SERIES, swaps)  4.15 us
    ppermute x1, starting transfers between devices, on_device(): far = lax.ppermute(to_far, SERIES, swaps)  3.84 us
    unnamed x10, local copies, waits for them, and re-layouts  2.64 us
  transfers between devices with their start and end apart: 2, of which 1 were waited for; matrix products, arithmetic and copies ran while one was open for 1% of the time, Pallas kernels for 17%

profile of v2, /device:TPU:64, one launch (start us, length us, event | category | flops | bytes accessed | tf_op | source)
XLA Modules:
  0.0 73.8 jit_solution(5048640114787238326)
XLA Ops:
  0.0 0.0 copy-start.1
  0.0 0.0 copy-start.3
  0.0 2.2 %cut.1 = bf16[384,1024]{1,0:T(8,128)(2,1)} custom-call(bf16[512,1024]{1,0:T(8,128)(2,1)} %bitcast.2), custom_call_target="tpu_custom_call" | custom-call | bytes 2097152 | tf_op jit(solution)/shard_map/cut/pallas_call | solution.py:349
  2.2 0.0 copy-done.1
  2.2 0.1 collective-permute-start.1
  2.3 3.8 %collective-permute-start = (bf16[384,1024]{1,0:T(8,128)(2,1)}, bf16[384,1024]{1,0:T(8,128)(2,1)S(1)}, u32[]{:S(2)}, u32[]{:S(2)}) collective-permute-start(bf16[384,1024]{1,0:T(8,128)(2,1)} %cut.1), channel_id=1, source_target_pairs={{8,16},{16,8},{24,32},{32,24},{40,48},{48,40},{56,64},{64,56},{72,... | collective-permute-start | bytes 2359304 | tf_op jit(solution)/shard_map/ppermute | solution.py:360
  6.2 0.3 fusion
  6.5 0.2 pad_maximum_fusion
  6.7 0.0 collective-permute-done.1.pair_ref
  6.7 0.0 copy-done.3
  6.7 0.0 copy-start.4
  6.7 1.2 %copy-done.4 = bf16[1024,512]{1,0:T(8,128)(2,1)S(1)} copy-done((bf16[1024,512]{1,0:T(8,128)(2,1)S(1)}, bf16[1024,512]{1,0:T(8,128)(2,1)}, u32[]{:S(2)}) %copy-start.4) | copy-done | bytes 1048600
  8.0 12.3 %own.1 = (bf16[512,512]{1,0:T(8,128)(2,1)S(1)}, bf16[896,512]{1,0:T(8,128)(2,1)S(1)}, bf16[896,512]{1,0:T(8,128)(2,1)S(1)}, bf16[512,1024]{1,0:T(8,128)(2,1)S(1)...) custom-call(s32[128]{0:T(128)S(1)} %copy-done.3, ...), custom_call_target="tpu_custom_call" | custom-call | flops 4563402752 | bytes 16777216 | tf_op jit(solution)/shard_map/own/pallas_call | solution.py:372
  20.3 4.1 %collective-permute-done.far_ref = bf16[384,1024]{1,0:T(8,128)(2,1)S(1)} collective-permute-done((bf16[384,1024]{1,0:T(8,128)(2,1)}, bf16[384,1024]{1,0:T(8,128)(2,1)S(1)}, u32[]{:S(2)}, u32[]{:S(2)}) %collective-permute-start) | collective-permute-done | bytes 786464 | tf_op jit(solution)/shard_map/ppermute | solution.py:360
  24.4 0.0 copy-start
  24.4 1.4 %copy-done = bf16[8,128,768]{2,1,0:T(8,128)(2,1)S(1)} copy-done((bf16[8,128,768]{2,1,0:T(8,128)(2,1)S(1)}, bf16[8,128,768]{2,1,0:T(8,128)(2,1)}, u32[]{:S(2)}) %copy-start) | copy-done | bytes 1572888
  25.8 5.9 %fix.1 = (bf16[512,1024]{1,0:T(8,128)(2,1)S(1)}, bf16[8,128,768]{2,1,0:T(8,128)(2,1)S(1)}) custom-call(s32[128]{0:T(128)S(1)} %copy-done.3, bf16[384,1024]{1,0:T(8,128)(2,1)S(1)} %collective-permute-done.far_ref, bf16[512,1024]{1,0:T(8,128)(2,1)S(1)} %bitcast.5, ...), custom_call_target="tpu_custom_call", output_to_operand_aliasing={{0}: (14, {}), {1}: (15, {})} | custom-call | flops 939524096 | bytes 4194304 | tf_op jit(solution)/shard_map/fix/pallas_call | solution.py:387
  31.8 22.5 %all_to_all.10.in_ref = bf16[8,128,768]{2,1,0:T(8,128)(2,1)S(1)} all-to-all(bf16[8,128,768]{2,1,0:T(8,128)(2,1)S(1)} %get-tuple-element.33), channel_id=1, replica_groups=mesh['zh'=4,'x'=4,'core'=2,'zl'=2,'y'=4] {'zl','y'}, dimensions={0} | all-to-all | bytes 3145728 | tf_op jit(solution)/shard_map/all_to_all | solution.py:406
  54.2 5.4 %time.1 = bf16[8,128,256]{2,1,0:T(8,128)(2,1)S(1)} custom-call(bf16[8,128,768]{2,1,0:T(8,128)(2,1)S(1)} %all_to_all.10.in_ref), custom_call_target="tpu_custom_call" | custom-call | flops 8589934592 | bytes 2097152 | tf_op jit(solution)/shard_map/time/pallas_call | solution.py:407
  59.6 0.0 copy-start.2
  59.6 12.5 %all_to_all.11.mixed_ref = bf16[8,128,256]{2,1,0:T(8,128)(2,1)S(1)} all-to-all(bf16[8,128,256]{2,1,0:T(8,128)(2,1)S(1)} %time.1), channel_id=1, replica_groups=mesh['zh'=4,'x'=4,'core'=2,'zl'=2,'y'=4] {'zl','y'}, dimensions={0} | all-to-all | bytes 1048576 | tf_op jit(solution)/shard_map/all_to_all | solution.py:417
  72.1 0.0 copy-done.2
  72.1 1.5 %out.1 = bf16[512,1024]{1,0:T(8,128)(2,1)} custom-call(bf16[8,128,256]{2,1,0:T(8,128)(2,1)S(1)} %all_to_all.11.mixed_ref, bf16[512,1024]{1,0:T(8,128)(2,1)S(1)} %get-tuple-element.34.mid_ref, bf16[512,1024]{1,0:T(8,128)(2,1)S(1)} %copy-done.2), custom_call_target="tpu_custom_call" | custom-call | flops 536870912 | bytes 4194304 | tf_op jit(solution)/shard_map/out/pallas_call | solution.py:418
  (2 shorter events, 0.0 us)
Async XLA Ops:
  0.0 2.2 %copy-start.1 = (bf16[4,128,1024]{2,1,0:T(8,128)(2,1)S(1)}, bf16[4,128,1024]{2,1,0:T(8,128)(2,1)}, u32[]{:S(2)}) copy-start(bf16[4,128,1024]{2,1,0:T(8,128)(2,1)} %param.10) | copy-start | bytes 3145732
  0.0 6.7 %copy-start.3 = (s32[128]{0:T(128)S(1)}, s32[128]{0:T(128)}, u32[]{:S(2)}) copy-start(s32[128]{0:T(128)} %ids_ref.3) | copy-start | bytes 1540
  2.2 4.5 %collective-permute-start.1 = (bf16[512,1024]{1,0:T(8,128)(2,1)S(1)}, bf16[512,1024]{1,0:T(8,128)(2,1)}, u32[]{:S(2)}, u32[]{:S(2)}) collective-permute-start(bf16[512,1024]{1,0:T(8,128)(2,1)S(1)} %bitcast.3), channel_id=1, source_target_pairs={{0,8},{8,0},{1,9},{9,1},{2,10},{10,2},{3,11},{11,3},{4,12},{12,4},... | collective-permute-start | bytes 3145736 | tf_op jit(solution)/shard_map/ppermute | solution.py:361
  2.3 22.1 %collective-permute-start = (bf16[384,1024]{1,0:T(8,128)(2,1)}, bf16[384,1024]{1,0:T(8,128)(2,1)S(1)}, u32[]{:S(2)}, u32[]{:S(2)}) collective-permute-start(bf16[384,1024]{1,0:T(8,128)(2,1)} %cut.1), channel_id=1, source_target_pairs={{8,16},{16,8},{24,32},{32,24},{40,48},{48,40},{56,64},{64,56},{72,... | collective-permute-start | bytes 2359304 | tf_op jit(solution)/shard_map/ppermute | solution.py:360
  6.7 1.2 %copy-start.4 = (bf16[1024,512]{1,0:T(8,128)(2,1)S(1)}, bf16[1024,512]{1,0:T(8,128)(2,1)}, u32[]{:S(2)}) copy-start(bf16[1024,512]{1,0:T(8,128)(2,1)} %wq_hbm.1) | copy-start | bytes 3145732
  24.4 1.4 %copy-start = (bf16[8,128,768]{2,1,0:T(8,128)(2,1)S(1)}, bf16[8,128,768]{2,1,0:T(8,128)(2,1)}, u32[]{:S(2)}) copy-start(bf16[8,128,768]{2,1,0:T(8,128)(2,1)} %get-tuple-element.32.send_in) | copy-start | bytes 4718596
  59.6 12.5 %copy-start.2 = (bf16[512,1024]{1,0:T(8,128)(2,1)S(1)}, bf16[512,1024]{1,0:T(8,128)(2,1)}, u32[]{:S(2)}) copy-start(bf16[512,1024]{1,0:T(8,128)(2,1)} %wo_ref.1) | copy-start | bytes 3145732
